TPU v7x, 32 devices: a whole 2x2x4 slice. The times are simulated.
32 devices in a mesh: replica: 4 (over y, x), fsdp: 8 (over z, core).
Axes of the slice: x: 2, y: 2, z: 4, core: 2. Of those that a mesh axis runs over, the one named last changes fastest.
Arguments:
- tokens: bfloat16 [4096, 2048], P(('replica', 'fsdp')), may hold values from -6 to 6
- attn_gain: bfloat16 [2048], P('fsdp'), may hold values from 0.5 to 1.5
- w_query: bfloat16 [2048, 2048], P('fsdp'), may hold values from -0.125 to 0.125
- w_key: bfloat16 [2048, 2048], P('fsdp'), may hold values from -0.125 to 0.125
- w_value: bfloat16 [2048, 2048], P('fsdp'), may hold values from -0.125 to 0.125
- w_out: bfloat16 [2048, 2048], P('fsdp'), may hold values from -0.75 to 0.75
- ffn_gain: bfloat16 [2048], P('fsdp'), may hold values from 0.5 to 1.5
- w_gate: bfloat16 [2048, 8192], P('fsdp'), may hold values from -0.125 to 0.125
- w_up: bfloat16 [2048, 8192], P('fsdp'), may hold values from -0.125 to 0.125
- w_down: bfloat16 [8192, 2048], P('fsdp'), may hold values from -0.0625 to 0.0625
- cotangent: bfloat16 [4096, 2048], P(('replica', 'fsdp')), may hold values from -6 to 6
Outputs:
- outputs: bfloat16 [4096, 2048], P(('replica', 'fsdp'))
- grad_tokens: float32 [4096, 2048], P(('replica', 'fsdp'))
- grad_attn_gain: float32 [2048], P('fsdp')
- grad_w_query: float32 [2048, 2048], P('fsdp')
- grad_w_key: float32 [2048, 2048], P('fsdp')
- grad_w_value: float32 [2048, 2048], P('fsdp')
- grad_w_out: float32 [2048, 2048], P('fsdp')
- grad_ffn_gain: float32 [2048], P('fsdp')
- grad_w_gate: float32 [2048, 8192], P('fsdp')
- grad_w_up: float32 [2048, 8192], P('fsdp')
- grad_w_down: float32 [8192, 2048], P('fsdp')
All inputs are finite; a program needn't handle non-finite values.
Results may differ from a plain program's by a relative error of at most 0.023.
Values may be sent and summed in bfloat16 or wider, within the bound.
A program may use at most 576 MiB of HBM per device.

v0:
```python
import functools

import jax
import jax.numpy as jnp
import numpy as np
from jax import lax
from jax.experimental import pallas as pl
from jax.experimental.pallas import tpu as pltpu
from jax.sharding import PartitionSpec as P

HEAD_DIM = 64

eps_norm = 1e-05
rope_base = 130000.0
masked_score = -1e30


def rope_tables(row_count):
    lane = np.arange(2 * HEAD_DIM) % HEAD_DIM
    halfway = HEAD_DIM // 2
    spacing = ((lane % halfway) * np.float32(2.0) / HEAD_DIM).astype(np.float32)
    frequency = np.power(np.float32(rope_base), -spacing)
    angles = np.arange(row_count, dtype=np.float32)[:, None] * frequency[None, :]
    sign = np.where(lane < halfway, -1.0, 1.0).astype(np.float32)
    return np.cos(angles).astype(np.float32), (np.sin(angles) * sign[None, :]).astype(np.float32)


def dot(left, right):
    return jnp.dot(left, right, preferred_element_type=jnp.float32)


def contract_last(left, right):
    return lax.dot_general(
        left, right, (((1,), (1,)), ((), ())), preferred_element_type=jnp.float32
    )


def contract_first(left, right):
    return lax.dot_general(
        left, right, (((0,), (0,)), ((), ())), preferred_element_type=jnp.float32
    )


def scores_of(queries, keys, first_row):
    rows, columns = queries.shape[0], keys.shape[0]
    scores = contract_last(queries, keys) * HEAD_DIM**-0.5
    at_row = lax.broadcasted_iota(jnp.int32, (rows, columns), 0) + first_row
    at_column = lax.broadcasted_iota(jnp.int32, (rows, columns), 1)
    return jnp.where(at_column <= at_row, scores, masked_score)


MESH = pl.DeviceIdType.MESH
VMEM_LIMIT = 61 * 2**20


def remote(src, dst, send, recv, **where):
    return pltpu.make_async_remote_copy(
        src_ref=src, dst_ref=dst, send_sem=send, recv_sem=recv, device_id=where, device_id_type=MESH
    )


def await_bytes(ref, sem):
    pltpu.make_async_copy(ref, ref, sem).wait()


def rows_at(ref, index, size):
    return ref.at[pl.ds(pl.multiple_of(index * size, size), size)]


class Place:
    def __init__(self):
        self.fsdp, self.replicas = lax.axis_size("fsdp"), lax.axis_size("replica")
        self.me, self.replica = lax.axis_index("fsdp"), lax.axis_index("replica")
        self.chips = self.fsdp // 2
        self.chip, self.core = self.me // 2, self.me % 2
        self.sibling = self.me + 1 - 2 * self.core
        self.high, self.wide = 2, self.replicas // 2
        self.a, self.b = self.replica // self.wide, self.replica % self.wide
        self.counts = ((self.wide, self.high), (self.high, self.wide))
        self.above = self.chip + 1 < self.chips
        self.below = self.chip >= 1

    def peer(self, half, stage, k):
        if half == stage:
            to = lax.rem(self.b + k, self.wide)
            return to, self.a * self.wide + to
        to = lax.rem(self.a + k, self.high)
        return to, to * self.wide + self.b

    def nearest(self, k):
        found = jnp.int32(0)
        for chip in range(self.chips):
            order = sorted(range(self.chips), key=lambda other, chip=chip: (abs(other - chip), other))
            found = found + jnp.where(self.chip == chip, order[k], 0)
        return found

    def enter(self):
        barrier = pltpu.get_barrier_semaphore()

        def greet(k, _):
            to = lax.rem(self.me + k, self.fsdp)
            pl.semaphore_signal(barrier, inc=1, device_id={"fsdp": to}, device_id_type=MESH)
            return 0

        def greet_replica(k, _):
            to = lax.rem(self.replica + k, self.replicas)
            pl.semaphore_signal(barrier, inc=1, device_id={"replica": to}, device_id_type=MESH)
            return 0

        lax.fori_loop(1, self.fsdp, greet, 0)
        lax.fori_loop(1, self.replicas, greet_replica, 0)
        pl.semaphore_wait(barrier, self.fsdp - 1 + self.replicas - 1)


def line_sems(chips):
    return [pltpu.SemaphoreType.DMA((chips,))] * 6


class Gather:
    def __init__(self, place, buf, block, sems, own=None):
        self.p, self.buf, self.block, self.own = place, buf, block, own
        self.up_out, self.up_in, self.down_out, self.down_in, self.side_out, self.side_in = sems

    def held(self, chip):
        return rows_at(self.buf, 2 * chip + self.p.core, self.block)

    def up(self, step):
        ref = self.held(self.p.chip - step + 1)
        src = self.own if step == 1 and self.own is not None else ref
        return remote(src, ref, self.up_out.at[step], self.up_in.at[step], fsdp=self.p.me + 2)

    def down(self, step):
        ref = self.held(self.p.chip + step - 1)
        src = self.own if step == 1 and self.own is not None else ref
        return remote(src, ref, self.down_out.at[step], self.down_in.at[step], fsdp=self.p.me - 2)

    def side(self, chip, src=None):
        ref = self.held(chip)
        src = ref if src is None else src
        return remote(src, ref, self.side_out.at[chip], self.side_in.at[chip], fsdp=self.p.sibling)

    def start(self):
        p = self.p
        pl.when(p.above)(lambda: self.up(1).start())
        pl.when(p.below)(lambda: self.down(1).start())
        self.side(p.chip, self.own).start()

    def step(self, step):
        p = self.p
        from_below, from_above = p.chip - step, p.chip + step

        @pl.when(from_below >= 0)
        def _():
            await_bytes(self.held(from_below), self.up_in.at[step])
            if step + 1 < p.chips:
                pl.when(p.above)(lambda: self.up(step + 1).start())
            self.side(from_below).start()

        @pl.when(from_above < p.chips)
        def _():
            await_bytes(self.held(from_above), self.down_in.at[step])
            if step + 1 < p.chips:
                pl.when(p.below)(lambda: self.down(step + 1).start())
            self.side(from_above).start()

    def across(self, chip):
        await_bytes(rows_at(self.buf, 2 * chip + 1 - self.p.core, self.block), self.side_in.at[chip])

    def drain(self):
        p = self.p
        for step in range(1, p.chips):
            pl.when(jnp.logical_and(p.above, p.chip - step + 1 >= 0))(
                lambda step=step: self.up(step).wait_send()
            )
            pl.when(jnp.logical_and(p.below, p.chip + step - 1 < p.chips))(
                lambda step=step: self.down(step).wait_send()
            )
        for chip in range(p.chips):
            self.side(chip).wait_send()

    def finish(self):
        for chip in range(self.p.chips):
            self.across(chip)
        self.drain()


class Scatter:
    def __init__(self, place, terms, across, slots, block, sems):
        self.p, self.terms, self.across, self.slots, self.block = place, terms, across, slots, block
        self.up_out, self.up_in, self.down_out, self.down_in, self.side_out, self.side_in = sems

    def side(self, chip):
        p = self.p
        return remote(
            rows_at(self.terms, 2 * chip + 1 - p.core, self.block),
            rows_at(self.across, chip, self.block),
            self.side_out.at[chip],
            self.side_in.at[chip],
            fsdp=p.sibling,
        )

    def term(self, chip):
        return rows_at(self.terms, 2 * chip + self.p.core, self.block)

    def up(self, step):
        return remote(
            self.term(self.p.chips - step + self.p.chip),
            self.slots.at[step - self.p.chip - 1],
            self.up_out.at[step],
            self.up_in.at[step],
            fsdp=self.p.me + 2,
        )

    def down(self, step):
        return remote(
            self.term(self.p.chip - self.p.chips + step),
            self.slots.at[step + 1],
            self.down_out.at[step],
            self.down_in.at[step],
            fsdp=self.p.me - 2,
        )

    def add(self, chip, arrived):
        term = self.term(chip)
        term[...] = (term[...].astype(jnp.float32) + arrived[...].astype(jnp.float32)).astype(term.dtype)

    def cross(self, chip):
        arrived = rows_at(self.across, chip, self.block)
        await_bytes(arrived, self.side_in.at[chip])
        self.add(chip, arrived)

    def step(self, step):
        p = self.p
        rising, falling = p.chips - step + p.chip, p.chip - p.chips + step

        @pl.when(jnp.logical_and(p.above, rising < p.chips))
        def _():
            if step > 1:

                @pl.when(p.below)
                def _():
                    arrived = self.slots.at[step - 1 - p.chip]
                    await_bytes(arrived, self.up_in.at[step - 1])
                    self.add(rising, arrived)

            self.up(step).start()

        @pl.when(jnp.logical_and(p.below, falling >= 0))
        def _():
            if step > 1:

                @pl.when(p.above)
                def _():
                    arrived = self.slots.at[step]
                    await_bytes(arrived, self.down_in.at[step - 1])
                    self.add(falling, arrived)

            self.down(step).start()

    def finish(self, total):
        p, last = self.p, self.p.chips - 1
        total[...] = self.term(p.chip)[...].astype(jnp.float32)

        @pl.when(p.below)
        def _():
            await_bytes(self.slots.at[last - p.chip], self.up_in.at[last])
            total[...] += self.slots[last - p.chip].astype(jnp.float32)

        @pl.when(p.above)
        def _():
            await_bytes(self.slots.at[last + 1], self.down_in.at[last])
            total[...] += self.slots[last + 1].astype(jnp.float32)

    def drain(self):
        p = self.p
        for step in range(1, p.chips):
            pl.when(jnp.logical_and(p.above, p.chips - step + p.chip < p.chips))(
                lambda step=step: self.up(step).wait_send()
            )
            pl.when(jnp.logical_and(p.below, p.chip - p.chips + step >= 0))(
                lambda step=step: self.down(step).wait_send()
            )
        for chip in range(p.chips):
            self.side(chip).wait_send()


def scatter_sems(chips):
    dma = pltpu.SemaphoreType.DMA
    return [dma((chips,))] * 6


class Turn:
    def __init__(self, place, weight, slab, first, sems):
        self.p, self.weight, self.slab, self.first = place, weight, slab, first
        self.far_out, self.far_in, self.near_out, self.near_in, self.own, self.passing = sems
        self.height, self.width = weight.shape[0], slab.shape[1]
        self.share = self.height // place.replicas

    def far_rows(self):
        return (self.p.fsdp - 2) * self.share

    def piece(self, block, share):
        at = self.first + block * self.height + share * self.share
        return self.slab.at[pl.ds(pl.multiple_of(at, self.share), self.share)]

    def whole(self, block):
        at = self.first + block * self.height
        return self.slab.at[pl.ds(pl.multiple_of(at, self.height), self.height)]

    def columns(self, to):
        return pl.ds(pl.multiple_of(to * self.width, self.width), self.width)

    def start(self):
        p = self.p

        def send(k, _):
            to = lax.rem(2 * p.chip + 2 + k, p.fsdp)
            share = pl.ds(pl.multiple_of(p.replica * self.share, self.share), self.share)
            remote(
                self.weight.at[share, self.columns(to)],
                self.piece(p.me, p.replica),
                self.far_out,
                self.far_in,
                fsdp=to,
            ).start()
            return 0

        lax.fori_loop(0, p.fsdp - 2, send, 0)
        self.near().start()
        self.mine().start()

    def near(self):
        p = self.p
        return remote(
            self.weight.at[:, self.columns(p.sibling)], self.whole(p.me), self.near_out, self.near_in, fsdp=p.sibling
        )

    def mine(self):
        return pltpu.make_async_copy(self.weight.at[:, self.columns(self.p.me)], self.whole(self.p.me), self.own)

    def await_far(self):
        await_bytes(self.slab.at[pl.ds(0, self.far_rows())], self.far_in)

    def bytes_of(self, pieces):
        return self.slab.at[pl.ds(0, pieces * self.share)]

    def pass_bytes(self, half, stage):
        first, second = self.p.counts[half]
        return self.bytes_of((self.p.chips - 1) * (second - 1 if stage == 0 else second * (first - 1)))

    def send_pieces(self, half, stage, shares):
        p = self.p

        def one(i, _):
            block = lax.rem(2 * p.chip + 2 + 2 * i + half, p.fsdp)
            for share in shares:
                ref = self.piece(block, share)
                for k in range(1, p.counts[half][1 - stage]):
                    _, replica = p.peer(half, 1 - stage, k)
                    remote(
                        ref,
                        ref,
                        self.passing.at[half, 2 * stage],
                        self.passing.at[half, 2 * stage + 1],
                        replica=replica,
                    ).start()
            return 0

        lax.fori_loop(0, p.chips - 1, one, 0)

    def pass_on(self):
        for half in range(2):
            self.send_pieces(half, 0, [self.p.replica])

    def pass_far(self):
        p = self.p
        for half in range(2):
            await_bytes(self.pass_bytes(half, 0), self.passing.at[half, 1])
            if half == 0:
                shares = [a * p.wide + p.b for a in range(p.high)]
            else:
                shares = [p.a * p.wide + b for b in range(p.wide)]
            self.send_pieces(half, 1, shares)

    def finish(self):
        for half in range(2):
            await_bytes(self.pass_bytes(half, 1), self.passing.at[half, 3])
        await_bytes(self.whole(self.p.sibling), self.near_in)
        self.mine().wait()

    def drain(self):
        await_bytes(self.slab.at[pl.ds(0, self.far_rows())], self.far_out)
        self.near().wait_send()
        for half in range(2):
            await_bytes(self.pass_bytes(half, 0), self.passing.at[half, 0])
            await_bytes(self.pass_bytes(half, 1), self.passing.at[half, 2])


def turn_sems():
    return [pltpu.SemaphoreType.DMA(())] * 5 + [pltpu.SemaphoreType.DMA((2, 4))]


def partner(values):
    halfway = HEAD_DIM // 2
    width = values.shape[1]
    lane = lax.broadcasted_iota(jnp.int32, values.shape, 1) % HEAD_DIM
    return jnp.where(
        lane < halfway,
        pltpu.roll(values, width - halfway, axis=1),
        pltpu.roll(values, halfway, axis=1),
    )


def front_kernel(
    tokens,
    cotangent,
    gain_one,
    gain_two,
    w_query,
    w_key,
    w_value,
    w_out,
    w_gate,
    w_up,
    w_down,
    cosine,
    sine,
    lowered_one,
    lowered_two_out,
    cotangents,
    slab_qkv_out,
    hidden_out,
    grad_gate_out,
    grad_up_out,
    terms_out,
    sums_out,
    queries,
    keys,
    values,
    attended,
    logs,
    after_attn,
    gains,
    low,
    tiles,
    lowered_two,
    slab_qkv,
    slab_gate,
    slab_up,
    held_down,
    terms,
    across,
    slots,
    tile_hidden,
    tile_gate,
    tile_up,
    tile_terms,
    tile_sums,
    gain_rows,
    gain_out,
    gain_in,
    copy_sems,
    load_sems,
    store_sems,
    *sems,
):
    place = Place()
    chips, block = place.chips, tokens.shape[0]
    model, width = tokens.shape[1], queries.shape[1]
    share = gain_one.shape[0]
    tile = 2 * block
    one_at, cot_at, two_at, scatter_at = sems[:6], sems[6:12], sems[12:18], sems[18:24]
    turn_at = [sems[24 + 6 * i : 30 + 6 * i] for i in range(5)]
    turns = [
        Turn(place, weight, slab_qkv, i * model, turn_at[i])
        for i, weight in enumerate((w_query, w_key, w_value))
    ]
    turn_gate = Turn(place, w_gate, slab_gate, 0, turn_at[3])
    turn_up = Turn(place, w_up, slab_up, 0, turn_at[4])
    here = pl.ds(pl.multiple_of(place.me * block, block), block)

    gain_rows[...] = jnp.zeros_like(gain_rows)
    gain_rows[0, :] = gain_one[...].astype(jnp.float32)
    gain_rows[1, :] = gain_two[...].astype(jnp.float32)
    load_down = pltpu.make_async_copy(w_down, held_down, copy_sems.at[0])
    load_down.start()
    keep_cot = pltpu.make_async_copy(cotangent, cotangents.at[here], copy_sems.at[1])
    keep_cot.start()
    place.enter()

    def send_gains(k, _):
        to = lax.rem(place.me + k, place.fsdp)
        remote(gain_rows, gains.at[place.me], gain_out, gain_in, fsdp=to).start()
        return 0

    lax.fori_loop(1, place.fsdp, send_gains, 0)
    for turn in turns:
        turn.start()
    gains[place.me] = gain_rows[...]
    inputs = tokens[...].astype(jnp.float32)
    factor = lax.rsqrt(jnp.mean(inputs * inputs, axis=-1, keepdims=True) + eps_norm)
    await_bytes(gains.at[pl.ds(0, place.fsdp - 1)], gain_in)
    for j in range(model // share):
        at = pl.ds(j * share, share)
        normed = tokens[:, at].astype(jnp.float32) * factor
        low[:, at] = (normed * gains[j, 0:1, :]).astype(jnp.bfloat16)
    first = Gather(place, lowered_one, block, one_at, low)
    first.start()
    keep_low = pltpu.make_async_copy(low, lowered_one.at[here], copy_sems.at[2])
    keep_low.start()
    for turn in turns:
        turn.await_far()
        turn.pass_on()
    for step in range(1, chips):
        if step == chips - 1:
            turn_gate.start()
        first.step(step)
        if step == 1:
            for turn in turns:
                turn.pass_far()
    turn_up.start()
    third = Gather(place, cotangents, block, cot_at, cotangent)
    third.start()
    keep_low.wait()
    first.finish()

    def load(source, t, slot):
        return pltpu.make_async_copy(rows_at(source, t, tile), tiles.at[slot], load_sems.at[slot])

    load(lowered_one, 0, 0).start()
    for turn in turns:
        turn.finish()
    keep_slab = pltpu.make_async_copy(slab_qkv, slab_qkv_out, copy_sems.at[3])
    keep_slab.start()
    for t in range(chips):
        if t + 1 < chips:
            load(lowered_one, t + 1, (t + 1) % 2).start()
        load(lowered_one, t, t % 2).wait()
        at = pl.ds(t * tile, tile)
        for i, ref in enumerate((queries, keys, values)):
            out = dot(tiles[t % 2], slab_qkv[i * model : (i + 1) * model, :])
            if i < 2:
                for j in range(0, width, 2 * HEAD_DIM):
                    pair = out[:, j : j + 2 * HEAD_DIM]
                    pair = pair * cosine[at, :] + partner(pair) * sine[at, :]
                    ref[at, j : j + 2 * HEAD_DIM] = pair.astype(jnp.bfloat16)
            else:
                ref[at, :] = out.astype(jnp.bfloat16)
    scatter = Scatter(place, terms, across, slots, block, scatter_at)
    pair = 2 * HEAD_DIM
    for t in range(chips):
        here_t, seen = pl.ds(t * tile, tile), pl.ds(0, (t + 1) * tile)

        def heads(h, _, t=t, here_t=here_t, seen=seen):
            lanes = pl.ds(pl.multiple_of(h * pair, pair), pair)
            q2, k2, v2 = queries[here_t, lanes], keys[seen, lanes], values[seen, lanes]
            mixed, stats = [], []
            for at in (0, HEAD_DIM):
                head = slice(at, at + HEAD_DIM)
                scores = scores_of(q2[:, head], k2[:, head], t * tile)
                most = jnp.max(scores, axis=-1, keepdims=True)
                weights = jnp.exp(scores - most)
                total = jnp.sum(weights, axis=-1, keepdims=True)
                mixed.append(dot((weights / total).astype(jnp.bfloat16), v2[:, head]))
                stats.append(jnp.broadcast_to(most + jnp.log(total), (tile, HEAD_DIM)))
            attended[here_t, lanes] = jnp.concatenate(mixed, axis=1).astype(jnp.bfloat16)
            logs[here_t, lanes] = jnp.concatenate(stats, axis=1)
            return 0

        lax.fori_loop(0, width // pair, heads, 0)
        terms[here_t, :] = dot(attended[here_t, :], w_out[...]).astype(jnp.bfloat16)
        scatter.side(t).start()
    for t in range(chips):
        scatter.cross(t)
    for step in range(1, chips):
        scatter.step(step)
        if step == 1:
            turn_gate.await_far()
            turn_gate.pass_on()
        if step < chips - 1:
            third.step(step)
        if step == 1:
            turn_gate.pass_far()
            turn_up.await_far()
            turn_up.pass_on()
        if step == max(chips - 2, 1):
            turn_up.pass_far()
    scatter.finish(after_attn)
    after_attn[...] += tokens[...].astype(jnp.float32)
    after = after_attn[...]
    factor = lax.rsqrt(jnp.mean(after * after, axis=-1, keepdims=True) + eps_norm)
    for j in range(model // share):
        at = pl.ds(j * share, share)
        normed = after_attn[:, at] * factor
        lowered_two[here, at] = (normed * gains[j, 1:2, :]).astype(jnp.bfloat16)
    second = Gather(place, lowered_two, block, two_at)
    second.start()
    third.step(chips - 1)
    keep_cot.wait()
    third.finish()
    load(cotangents, place.nearest(0), 0).start()
    turn_gate.finish()
    turn_up.finish()
    load_down.wait()

    def stores(k, t):
        slot = k % 2
        pairs = (
            (tile_hidden, hidden_out),
            (tile_gate, grad_gate_out),
            (tile_up, grad_up_out),
            (tile_terms, terms_out),
            (tile_sums, sums_out),
        )
        return [
            pltpu.make_async_copy(held.at[slot], rows_at(out, t, tile), store_sems.at[i, slot])
            for i, (held, out) in enumerate(pairs)
        ]

    for k in range(chips):
        t, slot = place.nearest(k), k % 2
        if k > 0:
            second.step(k)
        second.across(t)
        if k + 1 < chips:
            load(cotangents, place.nearest(k + 1), (k + 1) % 2).start()
        load(cotangents, t, slot).wait()
        if k > 1:
            for store in stores(k - 2, place.nearest(k - 2)):
                store.wait()
        rows = lowered_two[pl.ds(pl.multiple_of(t * tile, tile), tile), :]
        gate = dot(rows, slab_gate[...])
        up = dot(rows, slab_up[...])
        grad_hidden = contract_last(tiles[slot], held_down[...])
        sigmoid = jax.nn.sigmoid(gate)
        silu = gate * sigmoid
        hidden = (silu * up).astype(jnp.bfloat16)
        grad_gate = (grad_hidden * up * sigmoid * (1.0 + gate * (1.0 - sigmoid))).astype(jnp.bfloat16)
        grad_up = (grad_hidden * silu).astype(jnp.bfloat16)
        tile_hidden[slot] = hidden
        tile_gate[slot] = grad_gate
        tile_up[slot] = grad_up
        got = contract_last(grad_gate, slab_gate[...]) + contract_last(grad_up, slab_up[...])
        tile_terms[slot] = got.astype(jnp.bfloat16)
        tile_sums[slot] = dot(hidden, held_down[...]).astype(jnp.bfloat16)
        for store in stores(k, t):
            store.start()
    keep_two = pltpu.make_async_copy(lowered_two, lowered_two_out, copy_sems.at[4])
    keep_two.start()
    second.drain()
    scatter.drain()
    for turn in turns + [turn_gate, turn_up]:
        turn.drain()
    await_bytes(gains.at[pl.ds(0, place.fsdp - 1)], gain_out)
    keep_slab.wait()
    for k in range(max(chips - 2, 0), chips):
        for store in stores(k, place.nearest(k)):
            store.wait()
    keep_two.wait()


def front(
    tokens, cotangent, gain_one, gain_two, w_query, w_key, w_value, w_out, w_gate, w_up, w_down, cosine, sine
):
    fsdp = lax.axis_size("fsdp")
    chips = fsdp // 2
    block, model = tokens.shape
    rows, width, wide = fsdp * block, w_query.shape[1] // fsdp, w_gate.shape[1] // fsdp
    tile = 2 * block
    share = gain_one.shape[0]
    low, full = jnp.bfloat16, jnp.float32
    hbm, vmem = pl.BlockSpec(memory_space=pl.ANY), pl.BlockSpec(memory_space=pltpu.VMEM)
    shape = jax.ShapeDtypeStruct
    dma = pltpu.SemaphoreType.DMA
    return pl.pallas_call(
        front_kernel,
        in_specs=[vmem] * 4 + [hbm] * 3 + [vmem] + [hbm] * 3 + [vmem] * 2,
        out_specs=[hbm] * 9 + [vmem] * 7,
        out_shape=[
            shape((rows, model), low),
            shape((rows, model), low),
            shape((rows, model), low),
            shape((3 * model, width), low),
            shape((rows, wide), low),
            shape((rows, wide), low),
            shape((rows, wide), low),
            shape((rows, model), low),
            shape((rows, model), low),
            shape((rows, width), low),
            shape((rows, width), low),
            shape((rows, width), low),
            shape((rows, width), low),
            shape((rows, width), full),
            shape((block, model), full),
            shape((fsdp, 8, share), full),
        ],
        scratch_shapes=[
            pltpu.VMEM((block, model), low),
            pltpu.VMEM((2, tile, model), low),
            pltpu.VMEM((rows, model), low),
            pltpu.VMEM((3 * model, width), low),
            pltpu.VMEM((model, wide), low),
            pltpu.VMEM((model, wide), low),
            pltpu.VMEM((wide, model), low),
            pltpu.VMEM((rows, model), low),
            pltpu.VMEM((chips * block, model), low),
            pltpu.VMEM((chips + 1, block, model), low),
            pltpu.VMEM((2, tile, wide), low),
            pltpu.VMEM((2, tile, wide), low),
            pltpu.VMEM((2, tile, wide), low),
            pltpu.VMEM((2, tile, model), low),
            pltpu.VMEM((2, tile, model), low),
            pltpu.VMEM((8, share), full),
            dma(()),
            dma(()),
            dma((5,)),
            dma((2,)),
            dma((5, 2)),
        ]
        + line_sems(chips) * 3
        + scatter_sems(chips)
        + turn_sems() * 5,
        compiler_params=pltpu.CompilerParams(
            collective_id=0, has_side_effects=True, vmem_limit_bytes=VMEM_LIMIT
        ),
        name="front",
    )(
        tokens,
        cotangent,
        gain_one,
        gain_two,
        w_query,
        w_key,
        w_value,
        w_out,
        w_gate,
        w_up,
        w_down,
        cosine,
        sine,
    )


class Reduce:
    def __init__(self, place, part, first, second, sems):
        self.p, self.part, self.first, self.second, self.sems = place, part, first, second, sems
        self.half = part.shape[0] // 2

    def rows(self, half):
        return pl.ds(half * self.half, self.half)

    def sent(self, half, to):
        if half == 0:
            return self.part.at[self.rows(0), :, to]
        return self.part.at[self.rows(1), to]

    def own(self, half):
        return self.sent(half, self.p.b if half == 0 else self.p.a)

    def start(self, half):
        for k in range(1, self.p.counts[half][0]):
            to, replica = self.p.peer(half, 0, k)
            remote(
                self.sent(half, to),
                self.first[half].at[k - 1],
                self.sems.at[half, 0],
                self.sems.at[half, 1],
                replica=replica,
            ).start()

    def exchange(self):
        for half in range(2):
            own, arrived = self.own(half), self.first[half]
            await_bytes(arrived, self.sems.at[half, 1])

            def add(n, _, own=own, arrived=arrived):
                for m in range(own.shape[1]):
                    total = own[n, m].astype(jnp.float32)
                    for k in range(arrived.shape[0]):
                        total += arrived[k, n, m].astype(jnp.float32)
                    own[n, m] = total.astype(own.dtype)
                return 0

            lax.fori_loop(0, self.half, add, 0)
            for k in range(1, self.p.counts[half][1]):
                to, replica = self.p.peer(half, 1, k)
                remote(
                    own.at[:, to],
                    self.second[half].at[k - 1],
                    self.sems.at[half, 2],
                    self.sems.at[half, 3],
                    replica=replica,
                ).start()

    def total(self):
        for half in range(2):
            own, arrived = self.held(half), self.second[half]
            await_bytes(arrived, self.sems.at[half, 3])

            def add(n, _, own=own, arrived=arrived):
                total = own[n].astype(jnp.float32)
                for k in range(arrived.shape[0]):
                    total += arrived[k, n].astype(jnp.float32)
                own[n] = total.astype(own.dtype)
                return 0

            lax.fori_loop(0, self.half, add, 0)

    def held(self, half):
        return self.part.at[self.rows(half), self.p.a, self.p.b]

    def piece(self, n):
        return self.part.at[n, self.p.a, self.p.b]

    def drain(self):
        for half in range(2):
            await_bytes(self.first[half], self.sems.at[half, 0])
            await_bytes(self.second[half], self.sems.at[half, 2])


def reduce_scratch(n, high, wide, rows, columns):
    low = functools.partial(pltpu.VMEM, dtype=jnp.bfloat16)
    half = n // 2
    return [
        low((n, high, wide, rows, columns)),
        low((wide - 1, half, high, rows, columns)),
        low((high - 1, half, wide, rows, columns)),
        low((high - 1, half, rows, columns)),
        low((wide - 1, half, rows, columns)),
        pltpu.SemaphoreType.DMA((2, 4)),
    ]


def reducer(place, refs):
    part, first_a, first_b, second_a, second_b, sems = refs
    return Reduce(place, part, (first_a, first_b), (second_a, second_b), sems)


class Spread:
    def __init__(self, place, piece, out, sems, turned):
        self.p, self.piece, self.out, self.sems, self.turned = place, piece, out, sems, turned

    def start(self):
        p = self.p
        if self.turned:
            count = self.out.shape[0]
            width = self.out.shape[-1] // p.fsdp
            columns = pl.ds(pl.multiple_of(p.me * width, width), width)

            def pairs(to):
                ref = self.piece(to)
                return [
                    (ref.at[:, pl.ds(i * width, width)], self.out.at[i, p.a, p.b, :, columns])
                    for i in range(count)
                ]

            def send(k, _):
                to = lax.rem(p.me + k, p.fsdp)
                for ref, target in pairs(to):
                    remote(ref, target, self.sems.at[0, 0], self.sems.at[0, 1], fsdp=to).start()
                return 0

            lax.fori_loop(1, p.fsdp, send, 0)
            for ref, target in pairs(p.me):
                pltpu.make_async_copy(ref, target, self.sems.at[0, 1]).start()
        else:
            for half in range(2):
                pltpu.make_async_copy(
                    self.piece(half), self.out.at[half, p.a, p.b], self.sems.at[half, 1]
                ).start()

    def placed(self, half, rows):
        a, b = rows
        if self.turned:
            width = self.out.shape[-1] // 2
            return self.out.at[:, a, b, :, pl.ds(half * width, width)]
        return self.out.at[half, a, b]

    def spread(self):
        p = self.p
        if self.turned:
            await_bytes(self.out.at[:, p.a, p.b], self.sems.at[0, 1])
        for half in range(2):
            ref = self.placed(half, (p.a, p.b))
            src = ref if self.turned else self.piece(half)
            for k in range(1, p.counts[half][1]):
                _, replica = p.peer(half, 1, k)
                remote(src, ref, self.sems.at[half, 2], self.sems.at[half, 3], replica=replica).start()

    def spread_bytes(self, half):
        some = pl.ds(0, self.p.counts[half][1] - 1)
        return self.placed(half, (some, 0) if half == 0 else (0, some))

    def widen(self):
        p = self.p
        for half in range(2):
            if not self.turned:
                await_bytes(self.placed(half, (p.a, p.b)), self.sems.at[half, 1])
            await_bytes(self.spread_bytes(half), self.sems.at[half, 3])
            every = pl.ds(0, p.counts[half][1])
            ref = self.placed(half, (every, p.b) if half == 0 else (p.a, every))
            for k in range(1, p.counts[half][0]):
                _, replica = p.peer(half, 0, k)
                remote(ref, ref, self.sems.at[half, 4], self.sems.at[half, 5], replica=replica).start()

    def widen_bytes(self, half):
        counts = self.p.counts[half]
        every, some = pl.ds(0, counts[1]), pl.ds(0, counts[0] - 1)
        return self.placed(half, (every, some) if half == 0 else (some, every))

    def finish(self):
        p = self.p
        for half in range(2):
            await_bytes(self.widen_bytes(half), self.sems.at[half, 5])
            await_bytes(self.spread_bytes(half), self.sems.at[half, 2])
            await_bytes(self.widen_bytes(half), self.sems.at[half, 4])
        if self.turned:
            width = self.out.shape[-1] // p.fsdp
            await_bytes(
                self.out.at[:, p.a, p.b, :, pl.ds(0, (p.fsdp - 1) * width)], self.sems.at[0, 0]
            )


def spread_sems():
    return [pltpu.SemaphoreType.DMA((2, 6))]


def norm_back(values, gain_row, gains, grad, carried, result, gain_terms):
    block, model = values.shape
    share = gains.shape[2]
    held = values[...].astype(jnp.float32)
    factor = lax.rsqrt(jnp.mean(held * held, axis=-1, keepdims=True) + eps_norm)
    dots = jnp.zeros((block, 1), jnp.float32)
    for j in range(model // share):
        at = pl.ds(j * share, share)
        normed = values[:, at].astype(jnp.float32) * factor
        product = grad[:, at] * normed
        gain_terms[j, gain_row : gain_row + 1, :] = jnp.sum(product, axis=0, keepdims=True)
        dots += jnp.sum(product * gains[j, gain_row : gain_row + 1, :], axis=-1, keepdims=True)
    dots = dots / model
    for j in range(model // share):
        at = pl.ds(j * share, share)
        normed = values[:, at].astype(jnp.float32) * factor
        scaled = grad[:, at] * gains[j, gain_row : gain_row + 1, :]
        result[:, at] = carried[:, at].astype(jnp.float32) + factor * (scaled - normed * dots)


def weigh_kernel(
    cotangent,
    after_in,
    gains,
    terms_in,
    lowered_two,
    cotangents,
    hidden_in,
    grad_gate_in,
    grad_up_in,
    w_out_in,
    queries_in,
    keys_in,
    values_in,
    logs_in,
    cosine_in,
    sine_in,
    gain_terms,
    grad_after_out,
    grads_out,
    branch,
    sum_down,
    sum_gate,
    sum_up,
    after_attn,
    w_out,
    queries,
    keys,
    values,
    logs,
    cosine,
    sine,
    grad_after,
    grads,
    tokens_held,
    hidden,
    grad_gate,
    grad_up,
    terms,
    across,
    slots,
    summed,
    low,
    grad_low,
    grad_key,
    grad_value,
    load_sems,
    store_sems,
    late_sems,
    *rest,
):
    place = Place()
    chips, block = place.chips, cotangent.shape[0]
    model = cotangent.shape[1]
    tile = 2 * block
    scatter_at, gather_at = rest[:6], rest[6:12]
    down, gate, up = [reducer(place, rest[12 + 6 * i : 18 + 6 * i]) for i in range(3)]

    def load(t):
        at = pl.ds(t * tile, tile)
        return pltpu.make_async_copy(terms_in.at[at], terms.at[at], load_sems.at[t])

    loads = [
        pltpu.make_async_copy(source, target, load_sems.at[chips + i])
        for i, (source, target) in enumerate(
            (
                (cotangents, tokens_held),
                (hidden_in, hidden),
                (grad_gate_in, grad_gate),
                (grad_up_in, grad_up),
                (lowered_two, tokens_held),
            )
        )
    ]
    for t in range(chips):
        load(t).start()
    for copy in loads[:4]:
        copy.start()
    late = [
        pltpu.make_async_copy(source, target, late_sems.at[i])
        for i, (source, target) in enumerate(
            (
                (after_in, after_attn),
                (w_out_in, w_out),
                (queries_in, queries),
                (keys_in, keys),
                (values_in, values),
                (logs_in, logs),
                (cosine_in, cosine),
                (sine_in, sine),
            )
        )
    ]
    for copy in late:
        copy.start()
    keep_after = pltpu.make_async_copy(grad_after, grad_after_out, late_sems.at[8])
    keep_grads = pltpu.make_async_copy(grads, grads_out, late_sems.at[9])
    place.enter()
    scatter = Scatter(place, terms, across, slots, block, scatter_at)
    for t in range(chips):
        load(t).wait()
        scatter.side(t).start()
    gain_terms[...] = jnp.zeros_like(gain_terms)
    loads[0].wait()
    loads[1].wait()
    _, high, wide, thin, _ = down.part.shape
    columns = min(tile, hidden.shape[1])
    for i in range(0, hidden.shape[1], columns):
        got = contract_first(hidden[:, i : i + columns], tokens_held[...]).astype(jnp.bfloat16)
        for m in range(0, columns, thin):
            n = (i + m) // thin
            down.part[n // (high * wide), n // wide % high, n % wide] = got[m : m + thin, :]
        if 2 * (i + columns) == hidden.shape[1]:
            down.start(0)
    loads[4].start()
    down.start(1)
    for t in range(chips):
        scatter.cross(t)
    scatter.step(1)
    loads[4].wait()

    def weigh(reduce, grads):
        share = model // place.fsdp

        def rows(j, _):
            left = tokens_held[:, pl.ds(pl.multiple_of(j * share, share), share)]
            got = contract_first(left, grads[...]).astype(jnp.bfloat16)
            reduce.part[j] = got.reshape(reduce.part.shape[1:])
            return 0

        for half in range(2):
            lax.fori_loop(half * chips, (half + 1) * chips, rows, 0)
            reduce.start(half)

    loads[2].wait()
    weigh(gate, grad_gate)
    if chips > 2:
        scatter.step(2)
    loads[3].wait()
    weigh(up, grad_up)
    for step in range(3, chips):
        scatter.step(step)
    scatter.finish(summed)
    late[0].wait()
    norm_back(after_attn, 1, gains, summed, cotangent, grad_after, gain_terms)
    keep_after.start()
    low[...] = grad_after[...].astype(jnp.bfloat16)
    here = pl.ds(pl.multiple_of(place.me * block, block), block)
    gather = Gather(place, branch, block, gather_at, low)
    gather.start()
    keep = pltpu.make_async_copy(low, branch.at[here], store_sems.at[0])
    keep.start()
    scatter.drain()
    down.exchange()
    for step in range(1, chips):
        gather.step(step)
        if step == 1:
            gate.exchange()
        if step == max(chips - 2, 1):
            up.exchange()
    keep.wait()
    gather.finish()
    fetch = pltpu.make_async_copy(branch, tokens_held, load_sems.at[0])
    fetch.start()
    down.total()
    fetch.wait()
    for copy in late[1:]:
        copy.wait()

    def attend_rows(t, _):
        at = pl.ds(pl.multiple_of(t * tile, tile), tile)
        grad_low[at, :] = contract_last(tokens_held[at, :], w_out[...]).astype(jnp.bfloat16)
        return 0

    lax.fori_loop(0, chips, attend_rows, 0)
    width = queries.shape[1]
    scale = HEAD_DIM**-0.5
    grad_key[...] = jnp.zeros_like(grad_key)
    grad_value[...] = jnp.zeros_like(grad_value)
    pair = 2 * HEAD_DIM
    height = tile * 1024 // max(queries.shape[0], 1024)
    for first in range(0, queries.shape[0], height):
        rows, seen = pl.ds(first, height), pl.ds(0, first + height)

        def heads(h, _, first=first, rows=rows, seen=seen):
            lanes = pl.ds(pl.multiple_of(h * pair, pair), pair)
            q2, g2, log2 = queries[rows, lanes], grad_low[rows, lanes], logs[rows, lanes]
            k2, v2 = keys[seen, lanes], values[seen, lanes]
            for_queries, for_keys, for_values = [], [], []
            for at in (0, HEAD_DIM):
                head = slice(at, at + HEAD_DIM)
                q, g, k = q2[:, head], g2[:, head], k2[:, head]
                weights = jnp.exp(scores_of(q, k, first) - log2[:, at : at + 1])
                grad_weights = contract_last(g, v2[:, head])
                delta = jnp.sum(weights * grad_weights, axis=-1, keepdims=True)
                grad_scores = (weights * (grad_weights - delta)).astype(jnp.bfloat16)
                for_queries.append(dot(grad_scores, k))
                for_keys.append(contract_first(grad_scores, q))
                for_values.append(contract_first(weights.astype(jnp.bfloat16), g))
            got = jnp.concatenate(for_queries, axis=1) * scale
            got = got * cosine[rows, :] - partner(got) * sine[rows, :]
            grads[rows, lanes] = got.astype(jnp.bfloat16)
            grad_key[seen, lanes] += jnp.concatenate(for_keys, axis=1) * scale
            grad_value[seen, lanes] += jnp.concatenate(for_values, axis=1)
            return 0

        lax.fori_loop(0, width // pair, heads, 0)

    def turn_keys(t, _):
        at = pl.ds(pl.multiple_of(t * tile, tile), tile)
        for j in range(0, width, pair):
            got = grad_key[at, j : j + pair]
            got = got * cosine[at, :] - partner(got) * sine[at, :]
            grads[at, width + j : width + j + pair] = got.astype(jnp.bfloat16)
        grads[at, 2 * width :] = grad_value[at, :].astype(jnp.bfloat16)
        return 0

    lax.fori_loop(0, chips, turn_keys, 0)
    keep_grads.start()
    stores = [keep_after, keep_grads]
    for i, (reduce, out) in enumerate(((down, sum_down), (gate, sum_gate), (up, sum_up))):
        if i > 0:
            reduce.total()
        for half in range(2):
            store = pltpu.make_async_copy(
                reduce.held(half), out.at[reduce.rows(half)], store_sems.at[1 + 2 * i + half]
            )
            store.start()
            stores.append(store)
    for reduce in (down, gate, up):
        reduce.drain()
    for store in stores:
        store.wait()


def weigh(
    cotangent,
    after_attn,
    gains,
    terms,
    lowered_two,
    cotangents,
    hidden,
    grad_gate,
    grad_up,
    w_out,
    queries,
    keys,
    values,
    logs,
    cosine,
    sine,
):
    fsdp, replicas = lax.axis_size("fsdp"), lax.axis_size("replica")
    chips, high, wide = fsdp // 2, 2, replicas // 2
    block, model = cotangent.shape
    rows, columns = hidden.shape
    width = queries.shape[1]
    share = gains.shape[2]
    low, full = jnp.bfloat16, jnp.float32
    hbm, vmem = pl.BlockSpec(memory_space=pl.ANY), pl.BlockSpec(memory_space=pltpu.VMEM)
    shape = jax.ShapeDtypeStruct
    down_piece = (2, high, wide, columns // (2 * replicas), model)
    wide_piece = (fsdp, high, wide, share // replicas, columns)
    dma = pltpu.SemaphoreType.DMA
    return pl.pallas_call(
        weigh_kernel,
        in_specs=[vmem, hbm, vmem] + [hbm] * 13,
        out_specs=[vmem] + [hbm] * 6,
        out_shape=[
            shape((fsdp, 8, share), full),
            shape((block, model), full),
            shape((rows, 3 * width), low),
            shape((rows, model), low),
            shape((2,) + down_piece[3:], low),
            shape((fsdp,) + wide_piece[3:], low),
            shape((fsdp,) + wide_piece[3:], low),
        ],
        scratch_shapes=[
            pltpu.VMEM((block, model), full),
            pltpu.VMEM(w_out.shape, low),
            pltpu.VMEM((rows, width), low),
            pltpu.VMEM((rows, width), low),
            pltpu.VMEM((rows, width), low),
            pltpu.VMEM((rows, width), full),
            pltpu.VMEM(cosine.shape, full),
            pltpu.VMEM(sine.shape, full),
            pltpu.VMEM((block, model), full),
            pltpu.VMEM((rows, 3 * width), low),
            pltpu.VMEM((rows, model), low),
            pltpu.VMEM((rows, columns), low),
            pltpu.VMEM((rows, columns), low),
            pltpu.VMEM((rows, columns), low),
            pltpu.VMEM((rows, model), low),
            pltpu.VMEM((chips * block, model), low),
            pltpu.VMEM((chips + 1, block, model), low),
            pltpu.VMEM((block, model), full),
            pltpu.VMEM((block, model), low),
            pltpu.VMEM((rows, width), low),
            pltpu.VMEM((rows, width), full),
            pltpu.VMEM((rows, width), full),
            dma((chips + 5,)),
            dma((7,)),
            dma((10,)),
        ]
        + scatter_sems(chips)
        + line_sems(chips)
        + reduce_scratch(*down_piece)
        + reduce_scratch(*wide_piece)
        + reduce_scratch(*wide_piece),
        compiler_params=pltpu.CompilerParams(
            collective_id=1, has_side_effects=True, vmem_limit_bytes=VMEM_LIMIT
        ),
        name="weigh",
    )(
        cotangent,
        after_attn,
        gains,
        terms,
        lowered_two,
        cotangents,
        hidden,
        grad_gate,
        grad_up,
        w_out,
        queries,
        keys,
        values,
        logs,
        cosine,
        sine,
    )


def back_kernel(
    tokens,
    gains,
    grad_after_in,
    gain_terms_in,
    after_in,
    sums,
    sum_down,
    sum_gate,
    sum_up,
    branch_in,
    lowered_one,
    slab_in,
    attended_in,
    grads_in,
    outputs,
    grad_tokens,
    gain_out,
    out_down,
    out_gate,
    out_up,
    out_qkv,
    out_out,
    grad_after,
    after_attn,
    slab_qkv,
    attended,
    grads,
    terms,
    across,
    slots,
    branch,
    summed,
    gain_terms,
    gain_slots,
    gain_sums,
    gain_sems,
    load_sems,
    *rest,
):
    place = Place()
    chips, block = place.chips, tokens.shape[0]
    model, width = tokens.shape[1], attended.shape[1]
    share = gains.shape[2]
    tile = 2 * block
    scatter_at, rest = rest[:6], rest[6:]
    down = Spread(place, lambda n: sum_down.at[n], out_down, rest[0], False)
    gate = Spread(place, lambda n: sum_gate.at[n], out_gate, rest[1], True)
    up = Spread(place, lambda n: sum_up.at[n], out_up, rest[2], True)
    qkv, out = reducer(place, rest[5:11]), reducer(place, rest[11:17])
    qkv_spread = Spread(place, qkv.piece, out_qkv, rest[3], True)
    out_spread = Spread(place, out.piece, out_out, rest[4], False)
    load = pltpu.make_async_copy(lowered_one, branch, load_sems.at[0])
    load.start()
    loads = [
        pltpu.make_async_copy(source, target, load_sems.at[2 + i])
        for i, (source, target) in enumerate(
            (
                (grads_in, grads),
                (slab_in, slab_qkv),
                (attended_in, attended),
                (grad_after_in, grad_after),
                (after_in, after_attn),
            )
        )
    ]
    for copy in loads:
        copy.start()
    place.enter()
    down.start()
    down.spread()
    gate.start()
    load.wait()
    loads[0].wait()

    def weigh_rows(j, _):
        left = branch[:, pl.ds(pl.multiple_of(j * share, share), share)]
        got = contract_first(left, grads[...]).astype(jnp.bfloat16)
        qkv.part[j] = got.reshape(qkv.part.shape[1:])
        return 0

    for half in range(2):
        lax.fori_loop(half * chips, (half + 1) * chips, weigh_rows, 0)
        qkv.start(half)
    reload = pltpu.make_async_copy(branch_in, branch, load_sems.at[1])
    reload.start()
    scatter = Scatter(place, terms, across, slots, block, scatter_at)

    def back_rows(t, _):
        at = pl.ds(pl.multiple_of(t * tile, tile), tile)
        got = contract_last(grads[at, :width], slab_qkv[:model, :])
        got += contract_last(grads[at, width : 2 * width], slab_qkv[model : 2 * model, :])
        got += contract_last(grads[at, 2 * width :], slab_qkv[2 * model :, :])
        terms[at, :] = got.astype(jnp.bfloat16)
        return 0

    loads[1].wait()
    lax.fori_loop(0, chips, back_rows, 0)
    for t in range(chips):
        scatter.side(t).start()
    down.widen()
    reload.wait()
    loads[2].wait()
    _, high, wide, thin, columns = out.part.shape
    for half in range(2):
        for at in range(0, columns, 512):
            got = contract_first(
                attended[...], branch[:, half * columns + at : half * columns + at + 512]
            ).astype(jnp.bfloat16)
            out.part[half, :, :, :, at : at + 512] = got.reshape(high, wide, thin, 512)
    out.start(0)
    out.start(1)
    for t in range(chips):
        scatter.cross(t)
    scatter.step(1)
    gate.spread()
    qkv.exchange()
    for step in range(2, chips):
        scatter.step(step)
    up.start()
    scatter.finish(summed)
    gain_terms[...] = gain_terms_in[...]
    loads[3].wait()
    loads[4].wait()
    norm_back(tokens, 0, gains, summed, grad_after, grad_tokens, gain_terms)

    def send_gain(k, _):
        to = lax.rem(place.me + k, place.fsdp)
        remote(
            gain_terms.at[to], gain_slots.at[place.me], gain_sems.at[0], gain_sems.at[1], fsdp=to
        ).start()
        return 0

    lax.fori_loop(1, place.fsdp, send_gain, 0)
    gain_slots[place.me] = gain_terms[place.me]
    scatter.drain()
    load_sums = pltpu.make_async_copy(sums, terms, load_sems.at[0])
    load_sums.start()
    out.exchange()
    gate.widen()
    qkv.total()
    qkv_spread.start()
    await_bytes(gain_slots.at[pl.ds(0, place.fsdp - 1)], gain_sems.at[1])
    gain_sums[place.replica] = jnp.sum(gain_slots[...], axis=0)

    def send_sum(k, _):
        ref = gain_sums.at[place.replica]
        to = lax.rem(place.replica + k, place.replicas)
        remote(ref, ref, gain_sems.at[2], gain_sems.at[3], replica=to).start()
        return 0

    lax.fori_loop(1, place.replicas, send_sum, 0)

    load_sums.wait()
    for t in range(chips):
        scatter.side(t).start()
    up.spread()
    for t in range(chips):
        scatter.cross(t)
    scatter.step(1)
    out.total()
    out_spread.start()
    out_spread.spread()
    qkv_spread.spread()
    up.widen()
    for step in range(2, chips):
        scatter.step(step)
    out_spread.widen()
    scatter.finish(summed)
    outputs[...] = (summed[...] + after_attn[...]).astype(outputs.dtype)
    qkv_spread.widen()
    await_bytes(gain_sums.at[pl.ds(0, place.replicas - 1)], gain_sems.at[3])
    gain_out[...] = jnp.sum(gain_sums[...], axis=0)
    await_bytes(gain_slots.at[pl.ds(0, place.fsdp - 1)], gain_sems.at[0])
    await_bytes(gain_sums.at[pl.ds(0, place.replicas - 1)], gain_sems.at[2])
    scatter.drain()
    qkv.drain()
    out.drain()
    for spread in (down, gate, up, out_spread, qkv_spread):
        spread.finish()


def back(
    tokens,
    gains,
    grad_after,
    gain_terms,
    after_attn,
    sums,
    sum_down,
    sum_gate,
    sum_up,
    branch,
    lowered_one,
    slab_qkv,
    attended,
    grads,
):
    fsdp, replicas = lax.axis_size("fsdp"), lax.axis_size("replica")
    chips, high, wide = fsdp // 2, 2, replicas // 2
    block, model = tokens.shape
    rows, width = attended.shape
    share = gains.shape[2]
    low, full = jnp.bfloat16, jnp.float32
    hbm, vmem = pl.BlockSpec(memory_space=pl.ANY), pl.BlockSpec(memory_space=pltpu.VMEM)
    shape = jax.ShapeDtypeStruct
    thin = share // replicas
    columns = sum_gate.shape[-1]
    qkv_piece = (fsdp, high, wide, thin, 3 * width)
    out_piece = (2, high, wide, width // replicas, model // 2)
    dma = pltpu.SemaphoreType.DMA
    return pl.pallas_call(
        back_kernel,
        in_specs=[vmem, vmem, hbm, vmem] + [hbm] * 10,
        out_specs=[vmem] * 3 + [hbm] * 5,
        out_shape=[
            shape((block, model), low),
            shape((block, model), full),
            shape((8, share), full),
            shape((2, high, wide) + sum_down.shape[1:], low),
            shape((1, high, wide, thin, fsdp * columns), low),
            shape((1, high, wide, thin, fsdp * columns), low),
            shape((3, high, wide, thin, fsdp * width), low),
            shape(out_piece, low),
        ],
        scratch_shapes=[
            pltpu.VMEM((block, model), full),
            pltpu.VMEM((block, model), full),
            pltpu.VMEM(slab_qkv.shape, low),
            pltpu.VMEM((rows, width), low),
            pltpu.VMEM((rows, 3 * width), low),
            pltpu.VMEM((rows, model), low),
            pltpu.VMEM((chips * block, model), low),
            pltpu.VMEM((chips + 1, block, model), low),
            pltpu.VMEM((rows, model), low),
            pltpu.VMEM((block, model), full),
            pltpu.VMEM((fsdp, 8, share), full),
            pltpu.VMEM((fsdp, 8, share), full),
            pltpu.VMEM((replicas, 8, share), full),
            dma((4,)),
            dma((7,)),
        ]
        + scatter_sems(chips)
        + spread_sems() * 5
        + reduce_scratch(*qkv_piece)
        + reduce_scratch(*out_piece),
        compiler_params=pltpu.CompilerParams(
            collective_id=2, has_side_effects=True, vmem_limit_bytes=VMEM_LIMIT
        ),
        name="back",
    )(
        tokens,
        gains,
        grad_after,
        gain_terms,
        after_attn,
        sums,
        sum_down,
        sum_gate,
        sum_up,
        branch,
        lowered_one,
        slab_qkv,
        attended,
        grads,
    )


def widen_kernel(
    down,
    gate,
    up,
    qkv,
    out,
    outputs_in,
    tokens_in,
    gains,
    w_down,
    w_gate,
    w_up,
    w_query,
    w_key,
    w_value,
    w_out,
    outputs,
    grad_tokens,
    gain_one,
    gain_two,
):
    w_down[...] = down[...].astype(jnp.float32)
    w_gate[...] = gate[...].astype(jnp.float32)
    w_up[...] = up[...].astype(jnp.float32)
    for i, ref in enumerate((w_query, w_key, w_value)):
        ref[...] = qkv[i].astype(jnp.float32)
    half = out.shape[2]
    for i in range(2):
        w_out[:, i * half : (i + 1) * half] = out[i].astype(jnp.float32)
    outputs[...] = outputs_in[...]
    grad_tokens[...] = tokens_in[...]
    gain_one[...] = gains[0, :]
    gain_two[...] = gains[1, :]


def widen(down, gate, up, qkv, out, outputs, grad_tokens, gains):
    steps = min(16, gate.shape[0] // 16)
    token_steps = outputs.shape[0] // 16
    full = jnp.float32

    def rows(array):
        return pl.BlockSpec((array.shape[0] // steps, array.shape[1]), lambda i: (i, 0))

    def tokens(array):
        return pl.BlockSpec(
            (array.shape[0] // token_steps, array.shape[1]), lambda i: (jnp.minimum(i, token_steps - 1), 0)
        )

    def stacked(array):
        return pl.BlockSpec((array.shape[0], array.shape[1] // steps, array.shape[2]), lambda i: (0, i, 0))

    like = [down, gate, up, qkv[0], qkv[0], qkv[0]]
    shapes = [jax.ShapeDtypeStruct(array.shape, full) for array in like]
    shapes.append(jax.ShapeDtypeStruct((out.shape[1], 2 * out.shape[2]), full))
    row = jax.ShapeDtypeStruct(gains.shape[1:], full)
    whole = pl.BlockSpec(gains.shape, lambda i: (0, 0))
    line = pl.BlockSpec(gains.shape[1:], lambda i: (0,))
    return pl.pallas_call(
        widen_kernel,
        grid=(steps,),
        in_specs=[rows(down), rows(gate), rows(up), stacked(qkv), stacked(out)]
        + [tokens(outputs), tokens(grad_tokens), whole],
        out_specs=[rows(shape) for shape in shapes]
        + [tokens(outputs), tokens(grad_tokens), line, line],
        out_shape=shapes
        + [jax.ShapeDtypeStruct(array.shape, array.dtype) for array in (outputs, grad_tokens)]
        + [row, row],
        compiler_params=pltpu.CompilerParams(vmem_limit_bytes=VMEM_LIMIT),
        name="widen",
    )(down, gate, up, qkv, out, outputs, grad_tokens, gains)


def local(
    tokens, attn_gain, w_query, w_key, w_value, w_out, ffn_gain, w_gate, w_up, w_down, cotangent
):
    cosine, sine = rope_tables(tokens.shape[0] * lax.axis_size("fsdp"))
    (
        lowered_one,
        lowered_two,
        cotangents,
        slab_qkv,
        hidden,
        grad_gate,
        grad_up,
        terms,
        sums,
        queries,
        keys,
        values,
        attended,
        logs,
        after_attn,
        gains,
    ) = front(
        tokens,
        cotangent,
        attn_gain,
        ffn_gain,
        w_query,
        w_key,
        w_value,
        w_out,
        w_gate,
        w_up,
        w_down,
        cosine,
        sine,
    )
    gain_terms, grad_after, grads, branch, sum_down, sum_gate, sum_up = weigh(
        cotangent,
        after_attn,
        gains,
        terms,
        lowered_two,
        cotangents,
        hidden,
        grad_gate,
        grad_up,
        w_out,
        queries,
        keys,
        values,
        logs,
        cosine,
        sine,
    )
    outputs, grad_tokens, gain_grads, low_down, low_gate, low_up, low_qkv, low_out = back(
        tokens,
        gains,
        grad_after,
        gain_terms,
        after_attn,
        sums,
        sum_down,
        sum_gate,
        sum_up,
        branch,
        lowered_one,
        slab_qkv,
        attended,
        grads,
    )
    (
        grad_w_down,
        grad_w_gate,
        grad_w_up,
        grad_w_query,
        grad_w_key,
        grad_w_value,
        grad_w_out,
        outputs,
        grad_tokens,
        grad_attn_gain,
        grad_ffn_gain,
    ) = widen(
        low_down.reshape(w_down.shape),
        low_gate.reshape(w_gate.shape),
        low_up.reshape(w_up.shape),
        low_qkv.reshape((3,) + w_query.shape),
        low_out.reshape(2, w_out.shape[0], -1),
        outputs,
        grad_tokens,
        gain_grads,
    )
    return (
        outputs,
        grad_tokens,
        grad_attn_gain,
        grad_w_query,
        grad_w_key,
        grad_w_value,
        grad_w_out,
        grad_ffn_gain,
        grad_w_gate,
        grad_w_up,
        grad_w_down,
    )


def solution(mesh):
    rows = P("fsdp", None)
    tokens = P(("replica", "fsdp"), None)
    gain = P("fsdp")
    return jax.shard_map(
        local,
        mesh=mesh,
        in_specs=(tokens, gain, rows, rows, rows, rows, gain, rows, rows, rows, tokens),
        out_specs=(tokens, tokens, gain, rows, rows, rows, rows, gain, rows, rows, rows),
        check_vma=False,
    )
```

profile of v0, /device:TPU:0, one launch (start us, length us, event | category | flops | bytes accessed | tf_op | source)
XLA Modules:
  0.0 522.1 jit_solution(10275911017444284135)
XLA Ops:
  0.6 201.8 %front.1 = (bf16[1024,2048]{1,0:T(8,128)(2,1)}, bf16[1024,2048]{1,0:T(8,128)(2,1)}, bf16[1024,2048]{1,0:T(8,128)(2,1)}, bf16[6144,256]{1,0:T(8,128)(2,1)}, bf16[...) custom-call(bf16[128,2048]{1,0:T(8,128)(2,1)} %tokens.3, ...), custom_call_target="tpu_custom_call" | custom-call | tf_op jit(solution)/shard_map/front/pallas_call | solution.py:675
  202.4 116.9 %weigh.1 = (f32[8,8,256]{2,1,0:T(8,128)}, f32[128,2048]{1,0:T(8,128)}, bf16[1024,768]{1,0:T(8,128)(2,1)}, bf16[1024,2048]{1,0:T(8,128)(2,1)}, bf16[2,128,2048]{2...) custom-call(bf16[128,2048]{1,0:T(8,128)(2,1)} %cotangent.3, ...), custom_call_target="tpu_custom_call" | custom-call | tf_op jit(solution)/shard_map/weigh/pallas_call | solution.py:1213
  319.3 183.1 %back.1 = (bf16[128,2048]{1,0:T(8,128)(2,1)}, f32[128,2048]{1,0:T(8,128)}, f32[8,256]{1,0:T(8,128)}, bf16[2,2,2,128,2048]{4,3,2,1,0:T(8,128)(2,1)}, bf16[1,2,2,6...) custom-call(bf16[128,2048]{1,0:T(8,128)(2,1)} %tokens.3, ...), custom_call_target="tpu_custom_call" | custom-call | tf_op jit(solution)/shard_map/back/pallas_call | solution.py:1493
  502.4 19.4 %widen.1 = (f32[1024,2048]{1,0:T(8,128)}, f32[256,8192]{1,0:T(8,128)}, f32[256,8192]{1,0:T(8,128)}, f32[256,2048]{1,0:T(8,128)}, f32[256,2048]{1,0:T(8,128)}, /*...) custom-call(bf16[1024,2048]{1,0:T(8,128)(2,1)} %bitcast.5, ...), custom_call_target="tpu_custom_call" | custom-call | tf_op jit(solution)/shard_map/widen/pallas_call | solution.py:1607
where the time goes:
time: 531 us; the launch traced here: 522 us
  Pallas kernels  521 us (98%)
    pallas_call x1, Pallas kernels, front(): pl.pallas_call(front_kernel, in_specs=[vmem] * 4 + [hbm] * 3 + [vmem] + [...  202 us
    pallas_call x1, Pallas kernels, back(): pl.pallas_call(back_kernel, in_specs=[vmem, vmem, hbm, vmem] + [hbm] * 10...  183 us
    pallas_call x1, Pallas kernels, weigh(): pl.pallas_call(weigh_kernel, in_specs=[vmem, hbm, vmem] + [hbm] * 13, out...  117 us
    pallas_call x1, Pallas kernels, widen(): pl.pallas_call(widen_kernel, grid=(steps,), in_specs=[rows(down), rows(ga...  19.4 us

commit v1 on v0

--- a/solution.py
+++ b/solution.py
@@ -456,6 +456,7 @@
     tile_up,
     tile_terms,
     tile_sums,
+    grad_hiddens,
     gain_rows,
     gain_out,
     gain_in,
@@ -581,9 +582,10 @@
             third.step(step)
         if step == 1:
             turn_gate.pass_far()
+        if step == min(2, chips - 1):
             turn_up.await_far()
             turn_up.pass_on()
-        if step == max(chips - 2, 1):
+        if step == chips - 1:
             turn_up.pass_far()
     scatter.finish(after_attn)
     after_attn[...] += tokens[...].astype(jnp.float32)
@@ -599,9 +601,14 @@
     keep_cot.wait()
     third.finish()
     load(cotangents, place.nearest(0), 0).start()
+    load_down.wait()
+    for k in range(chips):
+        if k + 1 < chips:
+            load(cotangents, place.nearest(k + 1), (k + 1) % 2).start()
+        load(cotangents, place.nearest(k), k % 2).wait()
+        grad_hiddens[k] = contract_last(tiles[k % 2], held_down[...])
     turn_gate.finish()
     turn_up.finish()
-    load_down.wait()
 
     def stores(k, t):
         slot = k % 2
@@ -622,16 +629,13 @@
         if k > 0:
             second.step(k)
         second.across(t)
-        if k + 1 < chips:
-            load(cotangents, place.nearest(k + 1), (k + 1) % 2).start()
-        load(cotangents, t, slot).wait()
         if k > 1:
             for store in stores(k - 2, place.nearest(k - 2)):
                 store.wait()
         rows = lowered_two[pl.ds(pl.multiple_of(t * tile, tile), tile), :]
         gate = dot(rows, slab_gate[...])
         up = dot(rows, slab_up[...])
-        grad_hidden = contract_last(tiles[slot], held_down[...])
+        grad_hidden = grad_hiddens[k]
         sigmoid = jax.nn.sigmoid(gate)
         silu = gate * sigmoid
         hidden = (silu * up).astype(jnp.bfloat16)
@@ -710,6 +714,7 @@
             pltpu.VMEM((2, tile, wide), low),
             pltpu.VMEM((2, tile, model), low),
             pltpu.VMEM((2, tile, model), low),
+            pltpu.VMEM((chips, tile, wide), full),
             pltpu.VMEM((8, share), full),
             dma(()),
             dma(()),

time: 531 us -> 521 us (0.981)
  Pallas kernels: 521 us -> 511 us
    pallas_call x1, Pallas kernels: 202 us -> 193 us  [front(): pl.pallas_call(front_kernel, in_specs=[vmem] * 4 + [hbm] * 3 + [vmem] + [...]
where the time goes in v1:
time: 521 us; the launch traced here: 512 us
  Pallas kernels  511 us (98%)
    pallas_call x1, Pallas kernels, front(): pl.pallas_call(front_kernel, in_specs=[vmem] * 4 + [hbm] * 3 + [vmem] + [...  193 us
    pallas_call x1, Pallas kernels, back(): pl.pallas_call(back_kernel, in_specs=[vmem, vmem, hbm, vmem] + [hbm] * 10...  183 us
    pallas_call x1, Pallas kernels, weigh(): pl.pallas_call(weigh_kernel, in_specs=[vmem, hbm, vmem] + [hbm] * 13, out...  116 us
    pallas_call x1, Pallas kernels, widen(): pl.pallas_call(widen_kernel, grid=(steps,), in_specs=[rows(down), rows(ga...  19.4 us

profile of v1, /device:TPU:0, one launch (start us, length us, event | category | flops | bytes accessed | tf_op | source)
XLA Modules:
  0.0 512.0 jit_solution(11145225536067317895)
XLA Ops:
  0.6 192.8 %front.1 = (bf16[1024,2048]{1,0:T(8,128)(2,1)}, bf16[1024,2048]{1,0:T(8,128)(2,1)}, bf16[1024,2048]{1,0:T(8,128)(2,1)}, bf16[6144,256]{1,0:T(8,128)(2,1)}, bf16[...) custom-call(bf16[128,2048]{1,0:T(8,128)(2,1)} %tokens.3, ...), custom_call_target="tpu_custom_call" | custom-call | tf_op jit(solution)/shard_map/front/pallas_call | solution.py:679
  193.4 115.7 %weigh.1 = (f32[8,8,256]{2,1,0:T(8,128)}, f32[128,2048]{1,0:T(8,128)}, bf16[1024,768]{1,0:T(8,128)(2,1)}, bf16[1024,2048]{1,0:T(8,128)(2,1)}, bf16[2,128,2048]{2...) custom-call(bf16[128,2048]{1,0:T(8,128)(2,1)} %cotangent.3, ...), custom_call_target="tpu_custom_call" | custom-call | tf_op jit(solution)/shard_map/weigh/pallas_call | solution.py:1218
  309.1 183.1 %back.1 = (bf16[128,2048]{1,0:T(8,128)(2,1)}, f32[128,2048]{1,0:T(8,128)}, f32[8,256]{1,0:T(8,128)}, bf16[2,2,2,128,2048]{4,3,2,1,0:T(8,128)(2,1)}, bf16[1,2,2,6...) custom-call(bf16[128,2048]{1,0:T(8,128)(2,1)} %tokens.3, ...), custom_call_target="tpu_custom_call" | custom-call | tf_op jit(solution)/shard_map/back/pallas_call | solution.py:1498
  492.1 19.4 %widen.1 = (f32[1024,2048]{1,0:T(8,128)}, f32[256,8192]{1,0:T(8,128)}, f32[256,8192]{1,0:T(8,128)}, f32[256,2048]{1,0:T(8,128)}, f32[256,2048]{1,0:T(8,128)}, /*...) custom-call(bf16[1024,2048]{1,0:T(8,128)(2,1)} %bitcast.5, ...), custom_call_target="tpu_custom_call" | custom-call | tf_op jit(solution)/shard_map/widen/pallas_call | solution.py:1612

commit v2 on v1

--- a/solution.py
+++ b/solution.py
@@ -433,7 +433,6 @@
     grad_gate_out,
     grad_up_out,
     terms_out,
-    sums_out,
     queries,
     keys,
     values,
@@ -455,7 +454,6 @@
     tile_gate,
     tile_up,
     tile_terms,
-    tile_sums,
     grad_hiddens,
     gain_rows,
     gain_out,
@@ -617,7 +615,6 @@
             (tile_gate, grad_gate_out),
             (tile_up, grad_up_out),
             (tile_terms, terms_out),
-            (tile_sums, sums_out),
         )
         return [
             pltpu.make_async_copy(held.at[slot], rows_at(out, t, tile), store_sems.at[i, slot])
@@ -646,7 +643,6 @@
         tile_up[slot] = grad_up
         got = contract_last(grad_gate, slab_gate[...]) + contract_last(grad_up, slab_up[...])
         tile_terms[slot] = got.astype(jnp.bfloat16)
-        tile_sums[slot] = dot(hidden, held_down[...]).astype(jnp.bfloat16)
         for store in stores(k, t):
             store.start()
     keep_two = pltpu.make_async_copy(lowered_two, lowered_two_out, copy_sems.at[4])
@@ -679,7 +675,7 @@
     return pl.pallas_call(
         front_kernel,
         in_specs=[vmem] * 4 + [hbm] * 3 + [vmem] + [hbm] * 3 + [vmem] * 2,
-        out_specs=[hbm] * 9 + [vmem] * 7,
+        out_specs=[hbm] * 8 + [vmem] * 7,
         out_shape=[
             shape((rows, model), low),
             shape((rows, model), low),
@@ -688,7 +684,6 @@
             shape((rows, wide), low),
             shape((rows, wide), low),
             shape((rows, wide), low),
-            shape((rows, model), low),
             shape((rows, model), low),
             shape((rows, width), low),
             shape((rows, width), low),
@@ -712,7 +707,6 @@
             pltpu.VMEM((2, tile, wide), low),
             pltpu.VMEM((2, tile, wide), low),
             pltpu.VMEM((2, tile, wide), low),
-            pltpu.VMEM((2, tile, model), low),
             pltpu.VMEM((2, tile, model), low),
             pltpu.VMEM((chips, tile, wide), full),
             pltpu.VMEM((8, share), full),
@@ -1290,7 +1284,8 @@
     grad_after_in,
     gain_terms_in,
     after_in,
-    sums,
+    hidden_in,
+    w_down,
     sum_down,
     sum_gate,
     sum_up,
@@ -1312,6 +1307,7 @@
     slab_qkv,
     attended,
     grads,
+    hidden,
     terms,
     across,
     slots,
@@ -1347,6 +1343,7 @@
                 (attended_in, attended),
                 (grad_after_in, grad_after),
                 (after_in, after_attn),
+                (hidden_in, hidden),
             )
         )
     ]
@@ -1396,6 +1393,9 @@
             out.part[half, :, :, :, at : at + 512] = got.reshape(high, wide, thin, 512)
     out.start(0)
     out.start(1)
+    held_down = branch.at[pl.ds(0, w_down.shape[0])]
+    load_down = pltpu.make_async_copy(w_down, held_down, load_sems.at[0])
+    load_down.start()
     for t in range(chips):
         scatter.cross(t)
     scatter.step(1)
@@ -1420,8 +1420,6 @@
     lax.fori_loop(1, place.fsdp, send_gain, 0)
     gain_slots[place.me] = gain_terms[place.me]
     scatter.drain()
-    load_sums = pltpu.make_async_copy(sums, terms, load_sems.at[0])
-    load_sums.start()
     out.exchange()
     gate.widen()
     qkv.total()
@@ -1437,10 +1435,18 @@
 
     lax.fori_loop(1, place.replicas, send_sum, 0)
 
-    load_sums.wait()
+    up.spread()
+    load_down.wait()
+    loads[5].wait()
+
+    def sum_rows(t, _):
+        at = pl.ds(pl.multiple_of(t * tile, tile), tile)
+        terms[at, :] = dot(hidden[at, :], held_down[...]).astype(jnp.bfloat16)
+        return 0
+
+    lax.fori_loop(0, chips, sum_rows, 0)
     for t in range(chips):
         scatter.side(t).start()
-    up.spread()
     for t in range(chips):
         scatter.cross(t)
     scatter.step(1)
@@ -1472,7 +1478,8 @@
     grad_after,
     gain_terms,
     after_attn,
-    sums,
+    hidden,
+    w_down,
     sum_down,
     sum_gate,
     sum_up,
@@ -1497,7 +1504,7 @@
     dma = pltpu.SemaphoreType.DMA
     return pl.pallas_call(
         back_kernel,
-        in_specs=[vmem, vmem, hbm, vmem] + [hbm] * 10,
+        in_specs=[vmem, vmem, hbm, vmem] + [hbm] * 11,
         out_specs=[vmem] * 3 + [hbm] * 5,
         out_shape=[
             shape((block, model), low),
@@ -1515,6 +1522,7 @@
             pltpu.VMEM(slab_qkv.shape, low),
             pltpu.VMEM((rows, width), low),
             pltpu.VMEM((rows, 3 * width), low),
+            pltpu.VMEM(hidden.shape, low),
             pltpu.VMEM((rows, model), low),
             pltpu.VMEM((chips * block, model), low),
             pltpu.VMEM((chips + 1, block, model), low),
@@ -1524,7 +1532,7 @@
             pltpu.VMEM((fsdp, 8, share), full),
             pltpu.VMEM((replicas, 8, share), full),
             dma((4,)),
-            dma((7,)),
+            dma((8,)),
         ]
         + scatter_sems(chips)
         + spread_sems() * 5
@@ -1540,7 +1548,8 @@
         grad_after,
         gain_terms,
         after_attn,
-        sums,
+        hidden,
+        w_down,
         sum_down,
         sum_gate,
         sum_up,
@@ -1637,7 +1646,6 @@
         grad_gate,
         grad_up,
         terms,
-        sums,
         queries,
         keys,
         values,
@@ -1684,7 +1692,8 @@
         grad_after,
         gain_terms,
         after_attn,
-        sums,
+        hidden,
+        w_down,
         sum_down,
         sum_gate,
         sum_up,

time: 521 us -> 520 us (level)
  no operation moved by 1% of the time
where the time goes in v2:
time: 520 us; the launch traced here: 510 us
  Pallas kernels  509 us (98%)
    pallas_call x1, Pallas kernels, front(): pl.pallas_call(front_kernel, in_specs=[vmem] * 4 + [hbm] * 3 + [vmem] + [...  190 us
    pallas_call x1, Pallas kernels, back(): pl.pallas_call(back_kernel, in_specs=[vmem, vmem, hbm, vmem] + [hbm] * 11...  184 us
    pallas_call x1, Pallas kernels, weigh(): pl.pallas_call(weigh_kernel, in_specs=[vmem, hbm, vmem] + [hbm] * 13, out...  116 us
    pallas_call x1, Pallas kernels, widen(): pl.pallas_call(widen_kernel, grid=(steps,), in_specs=[rows(down), rows(ga...  19.4 us

profile of v2, /device:TPU:0, one launch (start us, length us, event | category | flops | bytes accessed | tf_op | source)
XLA Modules:
  0.0 510.0 jit_solution(6621512618034265352)
XLA Ops:
  0.6 189.7 %front.1 = (bf16[1024,2048]{1,0:T(8,128)(2,1)}, bf16[1024,2048]{1,0:T(8,128)(2,1)}, bf16[1024,2048]{1,0:T(8,128)(2,1)}, bf16[6144,256]{1,0:T(8,128)(2,1)}, bf16[...) custom-call(bf16[128,2048]{1,0:T(8,128)(2,1)} %tokens.3, ...), custom_call_target="tpu_custom_call" | custom-call | tf_op jit(solution)/shard_map/front/pallas_call | solution.py:675
  190.4 116.0 %weigh.1 = (f32[8,8,256]{2,1,0:T(8,128)}, f32[128,2048]{1,0:T(8,128)}, bf16[1024,768]{1,0:T(8,128)(2,1)}, bf16[1024,2048]{1,0:T(8,128)(2,1)}, bf16[2,128,2048]{2...) custom-call(bf16[128,2048]{1,0:T(8,128)(2,1)} %cotangent.3, ...), custom_call_target="tpu_custom_call" | custom-call | tf_op jit(solution)/shard_map/weigh/pallas_call | solution.py:1212
  306.3 183.7 %back.1 = (bf16[128,2048]{1,0:T(8,128)(2,1)}, f32[128,2048]{1,0:T(8,128)}, f32[8,256]{1,0:T(8,128)}, bf16[2,2,2,128,2048]{4,3,2,1,0:T(8,128)(2,1)}, bf16[1,2,2,6...) custom-call(bf16[128,2048]{1,0:T(8,128)(2,1)} %tokens.3, ...), custom_call_target="tpu_custom_call" | custom-call | tf_op jit(solution)/shard_map/back/pallas_call | solution.py:1505
  490.1 19.4 %widen.1 = (f32[1024,2048]{1,0:T(8,128)}, f32[256,8192]{1,0:T(8,128)}, f32[256,8192]{1,0:T(8,128)}, f32[256,2048]{1,0:T(8,128)}, f32[256,2048]{1,0:T(8,128)}, /*...) custom-call(bf16[1024,2048]{1,0:T(8,128)(2,1)} %bitcast.5, ...), custom_call_target="tpu_custom_call" | custom-call | tf_op jit(solution)/shard_map/widen/pallas_call | solution.py:1621
